TPU v7x, 32 devices: a whole 2x2x4 slice. The times are simulated.
32 devices in a mesh: grp: 8 (over y, x, core), qtr: 4 (over z).
Axes of the slice: x: 2, y: 2, z: 4, core: 2. Of those that a mesh axis runs over, the one named last changes fastest.
Arguments:
- vectors: float32 [8192, 512], P(('grp', 'qtr')), may hold values from -6 to 6
- previous: float32 [8192, 512], P(('grp', 'qtr')), may hold values from -6 to 6
- diag_tiles: bfloat16 [64, 4, 128, 128], P(('grp', 'qtr')), may hold values from -0.125 to 0.125
- diag_cols: int32 [64, 4], P(('grp', 'qtr')), may hold values from 0 to 7, all different within a row
- diag_mask: int32 [64, 4], P(('grp', 'qtr')), may hold values 0 or 1
- off_tiles: bfloat16 [3, 64, 4, 128, 128], P(None, ('grp', 'qtr')), may hold values from -0.125 to 0.125
- off_rows: int32 [3, 64, 4], P(None, ('grp', 'qtr')), may hold values from 0 to 7, all different within a row
- off_mask: int32 [3, 64, 4], P(None, ('grp', 'qtr')), may hold values 0 or 1
Outputs:
- chebyshev: float32 [8192, 512], P(('grp', 'qtr'))
Inputs may be any that keep to these rules, and one draw needn't show every extreme that they name: `diag_cols`: each row names 4 different tile columns of the group. `off_rows`: each row names 4 different tile rows of the group.
All inputs are finite; a program needn't handle non-finite values. No bound on the sum of `diag_mask` or of `off_mask` on one device may be relied on, other than what follows from the above.
Results may differ from a plain program's by a relative error of at most 0.002.
Values may be sent and summed in bfloat16 or wider, within the bound.
A program may use at most 64 MiB of HBM per device.

v0:
```python
import jax
import jax.numpy as jnp
from jax import lax
from jax.sharding import PartitionSpec as P

cheb_center = 0.25
cheb_half = 2.0


def from_partner(block, axis, bit):
    count = lax.axis_size(axis)
    route = []
    for low in range(count):
        high = low | 1 << bit
        if high != low and high < count:
            route += [(low, high), (high, low)]
    return lax.ppermute(block, axis, route)


def masked(tile_set, mask_ints):
    return tile_set * mask_ints[..., None, None].astype(jnp.bfloat16)


def spread_tiles(tile_set, targets, positions):
    select = (targets[None, :, :] == jnp.arange(positions, dtype=jnp.int32)[:, None, None]).astype(
        jnp.bfloat16
    )
    placed = jnp.einsum("gcs,csab->gcab", select, tile_set, preferred_element_type=jnp.float32)
    return placed.astype(jnp.bfloat16)


def on_device(vectors, previous, diag_tiles, diag_cols, diag_mask, off_tiles, off_rows, off_mask):
    tile_size = diag_tiles.shape[-1]
    strips = diag_tiles.shape[0]
    vec_width = vectors.shape[1]
    quarters = lax.axis_size("qtr")
    group_tiles = strips * quarters
    levels = lax.axis_size("grp").bit_length() - 1
    bit_list = [0, levels // 2, levels - 1]
    vec_bf = vectors.astype(jnp.bfloat16)
    own_tiles = vec_bf.reshape(strips, tile_size, vec_width)
    gathered = lax.all_gather(vec_bf, "qtr", axis=0, tiled=True).reshape(
        group_tiles, tile_size, vec_width
    )
    diag_live = masked(diag_tiles, diag_mask)
    picked = jnp.take(gathered, diag_cols, axis=0)
    result = jnp.einsum("tsab,tsbk->tak", diag_live, picked, preferred_element_type=jnp.float32)
    spread_list = [spread_tiles(jnp.swapaxes(diag_live, 2, 3), diag_cols, group_tiles)]
    operand_list = [own_tiles]
    off_live = masked(off_tiles, off_mask)
    arrivals = []
    for partner in range(3):
        arrived = from_partner(vec_bf, "grp", bit_list[partner])
        arrivals.append(arrived)
        spread_list.append(spread_tiles(off_live[partner], off_rows[partner], group_tiles))
        operand_list.append(arrived.reshape(strips, tile_size, vec_width))
    for partner in range(3):
        rows_picked = jnp.take(gathered, off_rows[partner], axis=0)
        outgoing = jnp.einsum(
            "csab,csak->cbk", off_live[partner], rows_picked, preferred_element_type=jnp.float32
        )
        result = result + from_partner(outgoing, "grp", bit_list[partner])
    spread_all = jnp.concatenate(spread_list, axis=1)
    operand_all = jnp.concatenate(operand_list, axis=0)
    group_terms = jnp.einsum(
        "gcab,cbk->gak", spread_all, operand_all, preferred_element_type=jnp.float32
    )
    group_terms = group_terms.reshape(group_tiles * tile_size, vec_width)
    summed = lax.psum_scatter(group_terms, "qtr", scatter_dimension=0, tiled=True)
    combined = result.reshape(strips * tile_size, vec_width) + summed
    return 2.0 / cheb_half * (combined - cheb_center * vectors) - previous


def solution(mesh):
    in_specs = (
        P(("grp", "qtr"), None),
        P(("grp", "qtr"), None),
        P(("grp", "qtr"), None, None, None),
        P(("grp", "qtr"), None),
        P(("grp", "qtr"), None),
        P(None, ("grp", "qtr"), None, None, None),
        P(None, ("grp", "qtr"), None),
        P(None, ("grp", "qtr"), None),
    )
    out_specs = P(("grp", "qtr"), None)
    return jax.shard_map(
        on_device, mesh=mesh, in_specs=in_specs, out_specs=out_specs, check_vma=False
    )
```

profile of v0, /device:TPU:0, one launch (start us, length us, event | category | flops | bytes accessed | tf_op | source)
XLA Modules:
  0.0 94.3 jit_solution(15958332932018212820)
XLA Ops:
  6.5 1.1 %convert_element_type.40 = bf16[256,512]{1,0:T(8,128)(2,1)S(1)} convert(f32[256,512]{1,0:T(8,128)} %param.10) | non-fusion elementwise | flops 131072 | bytes 786432 | tf_op jit(solution)/shard_map/convert_element_type | solution.py:40
  7.6 0.5 collective-permute-start.3
  8.2 2.6 %collective-permute-start.4 = (bf16[256,512]{1,0:T(8,128)(2,1)S(1)}, bf16[256,512]{1,0:T(8,128)(2,1)}, u32[]{:S(2)}, u32[]{:S(2)}) collective-permute-start(bf16[256,512]{1,0:T(8,128)(2,1)S(1)} %convert_element_type.40), channel_id=1, source_target_pairs={{0,8},{8,0},{4,12},{12,4},{16,24},{24,16},{20,28},{28,20},{1,9},{9... | collective-permute-start | bytes 786440 | tf_op jit(solution)/shard_map/ppermute | solution.py:17
  10.7 1.5 %collective-permute-start.5 = (bf16[256,512]{1,0:T(8,128)(2,1)S(1)}, bf16[256,512]{1,0:T(8,128)(2,1)}, u32[]{:S(2)}, u32[]{:S(2)}) collective-permute-start(bf16[256,512]{1,0:T(8,128)(2,1)S(1)} %convert_element_type.40), channel_id=1, source_target_pairs={{0,16},{16,0},{4,20},{20,4},{8,24},{24,8},{12,28},{28,12},{1,17},{... | collective-permute-start | bytes 786440 | tf_op jit(solution)/shard_map/ppermute | solution.py:17
  12.2 0.0 all-gather.2.cloned.1.call-update
  12.3 0.0 reduce-scatter.2.cloned.1.call-start
  12.3 1.5 %copy.9 = bf16[3,2,4,128,128]{3,4,2,1,0:T(8,128)(2,1)S(1)} copy(bf16[3,2,4,128,128]{4,3,2,1,0:T(8,128)(2,1)} %param.15) | data formatting | bytes 1572864 | tf_op args[5]
  13.9 0.1 broadcast_multiply_fusion
  14.0 0.1 slice_bitcast_fusion.2
  14.1 0.2 copy.20
  14.3 0.3 copy-done.6
  14.6 0.3 fusion.39
  14.8 0.0 copy-start.9
  14.9 0.0 copy-start.2
  14.9 0.1 copy.47
  15.0 0.2 copy.23
  15.2 0.3 fusion.37
  15.5 0.1 copy.48
  15.6 0.2 copy.17
  15.8 0.0 copy-done.2
  15.8 0.1 multiply_bitcast_fusion
  15.9 0.2 copy.14
  16.2 0.3 fusion.41
  16.5 0.3 fusion.43
  16.7 0.1 fusion.25
  16.9 0.8 collective-permute-done.4
  17.7 1.5 %collective-permute-done.5 = bf16[256,512]{1,0:T(8,128)(2,1)} collective-permute-done((bf16[256,512]{1,0:T(8,128)(2,1)S(1)}, bf16[256,512]{1,0:T(8,128)(2,1)}, u32[]{:S(2)}, u32[]{:S(2)}) %collective-permute-start.5) | collective-permute-done | bytes 262176 | tf_op jit(solution)/shard_map/ppermute | solution.py:17
  19.2 3.8 %fusion = f32[8,128,512,1]{2,1,3,0:T(8,128)} fusion(bf16[8,2,128,128]{3,2,1,0:T(8,128)(2,1)S(1)} %bitcast.102, bf16[8,2,128,128]{3,2,1,0:T(8,128)(2,1)S(1)} %bitcast.101, bf16[8,2,128,128]{3,2,1,0:T(8,128)(2,1)S(1)} %get-tuple-element.21, bf16[8,2,128,128]{3,2,1,0:T(8,128)(2,1)S(1)} %get-tuple-element.20, bf16[2,128,512]{2,1,0:T(8,128)(2,1)} %bitcast.32, ...), kind=kOutput, calls=%fused_computation.4 | convolution fusion | flops 1078460416 | bytes 5242880 | tf_op jit(solution)/shard_map/gcab,cbk->gak/dot_general | solution.py:65
  23.0 0.0 reduce-scatter.2.cloned.1.call-update
  23.0 0.1 reshape.82
  23.1 0.1 reshape.86
  23.2 0.1 reshape.90
  23.3 16.4 %all-gather.2.cloned.1.call-done = bf16[1024,512]{1,0:T(8,128)(2,1)} async-done(((bf16[256,512]{1,0:T(8,128)(2,1)}), bf16[1024,512]{1,0:T(8,128)(2,1)}) %all-gather.2.cloned.1.call-update) | async-done | bytes 1048592 | tf_op jit(solution)/shard_map/all_gather | solution.py:42
  39.7 1.9 %gather_fusion.1 = bf16[8,128,512]{2,1,0:T(8,128)(2,1)S(1)} fusion(bf16[8,128,512]{2,1,0:T(8,128)(2,1)} %bitcast.91, s32[1024]{0:T(1024)S(1)} %pad_clamp_fusion.2), kind=kCustom, calls=%fused_computation.1.clone | custom fusion | bytes 2097184 | tf_op jit(solution)/shard_map/jit(_take)/gather | solution.py:58
  41.7 1.2 %convolution_bitcast_fusion.2 = f32[2,128,512]{2,1,0:T(8,128)} fusion(bf16[2,4,128,512]{3,2,1,0:T(8,128)(2,1)S(1)} %bitcast.99, pred[2,4]{1,0:T(4,128)(4,1)S(1)} %get-tuple-element.9, bf16[3,2,4,128,128]{3,4,2,1,0:T(8,128)(2,1)S(1)} %broadcast_multiply_fusion), kind=kOutput, calls=%fused_computation.14 | convolution fusion | flops 134742016 | bytes 1835520 | tf_op jit(solution)/shard_map/csab,csak->cbk/dot_general | solution.py:59
  42.9 0.6 gather_fusion.2
  43.5 1.2 %convolution_bitcast_fusion.1 = f32[2,128,512]{2,1,0:T(8,128)} fusion(bf16[2,4,128,512]{3,2,1,0:T(8,128)(2,1)S(1)} %bitcast.100, pred[2,4]{1,0:T(4,128)(4,1)S(1)} %get-tuple-element.11, bf16[3,2,4,128,128]{3,4,2,1,0:T(8,128)(2,1)S(1)} %broadcast_multiply_fusion), kind=kOutput, calls=%fused_computation.13 | convolution fusion | flops 134742016 | bytes 1835520 | tf_op jit(solution)/shard_map/csab,csak->cbk/dot_general | solution.py:59
  44.7 1.5 %collective-permute-start.1 = (f32[2,128,512]{2,1,0:T(8,128)}, f32[2,128,512]{2,1,0:T(8,128)}, u32[]{:S(2)}, u32[]{:S(2)}) collective-permute-start(f32[2,128,512]{2,1,0:T(8,128)} %convolution_bitcast_fusion.1), channel_id=1, source_target_pairs={{0,8},{8,0},{4,12},{12,4},{16,24},{24,16},{20,28},{28,20},{1,9},{9... | collective-permute-start | bytes 1572872 | tf_op jit(solution)/shard_map/ppermute | solution.py:17
  46.1 0.6 gather_fusion.3
  46.7 1.2 %convolution_bitcast_fusion = f32[2,128,512]{2,1,0:T(8,128)} fusion(bf16[2,4,128,512]{3,2,1,0:T(8,128)(2,1)S(1)} %bitcast.98, pred[2,4]{1,0:T(4,128)(4,1)S(1)} %get-tuple-element.10, bf16[3,2,4,128,128]{3,4,2,1,0:T(8,128)(2,1)S(1)} %broadcast_multiply_fusion), kind=kOutput, calls=%fused_computation.12 | convolution fusion | flops 134742016 | bytes 1835520 | tf_op jit(solution)/shard_map/csab,csak->cbk/dot_general | solution.py:59
  47.9 1.5 %collective-permute-start.2 = (f32[2,128,512]{2,1,0:T(8,128)}, f32[2,128,512]{2,1,0:T(8,128)}, u32[]{:S(2)}, u32[]{:S(2)}) collective-permute-start(f32[2,128,512]{2,1,0:T(8,128)} %convolution_bitcast_fusion), channel_id=1, source_target_pairs={{0,16},{16,0},{4,20},{20,4},{8,24},{24,8},{12,28},{28,12},{1,17},{... | collective-permute-start | bytes 1572872 | tf_op jit(solution)/shard_map/ppermute | solution.py:17
  49.4 0.1 reshape.78
  49.5 0.6 gather_fusion
  50.2 9.2 %collective-permute-done.1 = f32[2,128,512]{2,1,0:T(8,128)} collective-permute-done((f32[2,128,512]{2,1,0:T(8,128)}, f32[2,128,512]{2,1,0:T(8,128)}, u32[]{:S(2)}, u32[]{:S(2)}) %collective-permute-start.1) | collective-permute-done | bytes 524320 | tf_op jit(solution)/shard_map/ppermute | solution.py:17
  59.3 3.0 %collective-permute-done.2 = f32[2,128,512]{2,1,0:T(8,128)} collective-permute-done((f32[2,128,512]{2,1,0:T(8,128)}, f32[2,128,512]{2,1,0:T(8,128)}, u32[]{:S(2)}, u32[]{:S(2)}) %collective-permute-start.2) | collective-permute-done | bytes 524320 | tf_op jit(solution)/shard_map/ppermute | solution.py:17
  62.3 1.8 %fusion.10 = f32[2,128,512]{2,1,0:T(8,128)S(1)} fusion(f32[2,128,512]{2,1,0:T(8,128)} %collective-permute-done.2, f32[2,128,512]{2,1,0:T(8,128)} %collective-permute-done.1, f32[2,128,512]{2,1,0:T(8,128)} %collective-permute-done, bf16[2,4,128,512]{3,2,1,0:T(8,128)(2,1)S(1)} %bitcast.95, pred[2,4]{1,0:T(4,128)(4,1)S(1)} %compare_and_fusion.3, ...), kind=kOutput, calls=%fused_computation.18 | convolution fusion | flops 135266304 | bytes 3407896 | tf_op jit(solution)/shard_map/tsab,tsbk->tak/dot_general | solution.py:47
  64.1 21.3 %reduce-scatter.2.cloned.1.call-done = f32[256,512]{1,0:T(8,128)} async-done(((f32[1024,512]{1,0:T(8,128)}), f32[256,512]{1,0:T(8,128)}) %reduce-scatter.2.cloned.1.call-update) | async-done | bytes 524304 | tf_op jit(solution)/shard_map/reduce_scatter | solution.py:69
  85.4 2.0 %fusion.30 = f32[256,512]{1,0:T(8,128)} fusion(f32[256,512]{1,0:T(8,128)S(1)} %copy-done.5, f32[256,512]{1,0:T(8,128)} %reduce-scatter.2.cloned.1.call-done, f32[2,128,512]{2,1,0:T(8,128)S(1)} %fusion.10, f32[256,512]{1,0:T(8,128)S(1)} %copy-done.1), kind=kLoop, calls=%fused_computation.44 | loop fusion | flops 524288 | bytes 2621440 | tf_op jit(solution)/shard_map/sub | solution.py:71
  (34 shorter events, 0.1 us)
Async XLA Ops:
  6.5 7.3 %copy-start.8 = (s32[3,2,4]{2,1,0:T(2,128)S(1)}, s32[3,2,4]{2,1,0:T(2,128)}, u32[]{:S(2)}) copy-start(s32[3,2,4]{2,1,0:T(2,128)} %param.17) | copy-start | bytes 292
  6.5 33.2 %all-gather.2.cloned.1.call-start = ((), (), s32[]{:S(2)}) async-start(), calls=%async_computation.1 | async-start | bytes 1310720 | tf_op jit(solution)/shard_map/all_gather | solution.py:42
  7.6 4.6 %copy-start.3 = (bf16[256,512]{1,0:T(8,128)(2,1)}, bf16[256,512]{1,0:T(8,128)(2,1)S(1)}, u32[]{:S(2)}) copy-start(bf16[256,512]{1,0:T(8,128)(2,1)S(1)} %convert_element_type.40) | copy-start | bytes 786436
  7.6 9.3 %collective-permute-start.3 = (bf16[256,512]{1,0:T(8,128)(2,1)S(1)}, bf16[256,512]{1,0:T(8,128)(2,1)}, u32[]{:S(2)}, u32[]{:S(2)}) collective-permute-start(bf16[256,512]{1,0:T(8,128)(2,1)S(1)} %convert_element_type.40), channel_id=1, source_target_pairs={{0,4},{4,0},{8,12},{12,8},{16,20},{20,16},{24,28},{28,24},{1,5},{5... | collective-permute-start | bytes 786440 | tf_op jit(solution)/shard_map/ppermute | solution.py:17
  8.2 9.6 %collective-permute-start.4 = (bf16[256,512]{1,0:T(8,128)(2,1)S(1)}, bf16[256,512]{1,0:T(8,128)(2,1)}, u32[]{:S(2)}, u32[]{:S(2)}) collective-permute-start(bf16[256,512]{1,0:T(8,128)(2,1)S(1)} %convert_element_type.40), channel_id=1, source_target_pairs={{0,8},{8,0},{4,12},{12,4},{16,24},{24,16},{20,28},{28,20},{1,9},{9... | collective-permute-start | bytes 786440 | tf_op jit(solution)/shard_map/ppermute | solution.py:17
  10.7 8.5 %collective-permute-start.5 = (bf16[256,512]{1,0:T(8,128)(2,1)S(1)}, bf16[256,512]{1,0:T(8,128)(2,1)}, u32[]{:S(2)}, u32[]{:S(2)}) collective-permute-start(bf16[256,512]{1,0:T(8,128)(2,1)S(1)} %convert_element_type.40), channel_id=1, source_target_pairs={{0,16},{16,0},{4,20},{20,4},{8,24},{24,8},{12,28},{28,12},{1,17},{... | collective-permute-start | bytes 786440 | tf_op jit(solution)/shard_map/ppermute | solution.py:17
  12.3 73.1 %reduce-scatter.2.cloned.1.call-start = ((), (), s32[]{:S(2)}) async-start(), calls=%async_computation.2 | async-start | bytes 2621440 | tf_op jit(solution)/shard_map/reduce_scatter | solution.py:69
  13.8 0.7 copy-start.6
  14.8 0.9 copy-start.9
  14.9 1.0 %copy-start.2 = (bf16[2,4,128,128]{3,2,1,0:T(8,128)(2,1)S(1)}, bf16[2,4,128,128]{3,2,1,0:T(8,128)(2,1)}, u32[]{:S(2)}) copy-start(bf16[2,4,128,128]{3,2,1,0:T(8,128)(2,1)} %param.12) | copy-start | bytes 786436
  15.0 1.2 %copy-start.7 = (s32[2,4]{1,0:T(2,128)S(1)}, s32[2,4]{1,0:T(2,128)}, u32[]{:S(2)}) copy-start(s32[2,4]{1,0:T(2,128)} %param.13) | copy-start | bytes 100
  15.9 3.3 %copy-start.4 = (bf16[256,512]{1,0:T(8,128)(2,1)S(1)}, bf16[256,512]{1,0:T(8,128)(2,1)}, u32[]{:S(2)}) copy-start(bf16[256,512]{1,0:T(8,128)(2,1)} %copy-done.3) | copy-start | bytes 786436
  39.7 3.1 %copy-start = (bf16[1024,512]{1,0:T(8,128)(2,1)S(1)}, bf16[1024,512]{1,0:T(8,128)(2,1)}, u32[]{:S(2)}) copy-start(bf16[1024,512]{1,0:T(8,128)(2,1)} %all-gather.2.cloned.1.call-done) | copy-start | bytes 3145732
  42.8 7.3 %collective-permute-start = (f32[2,128,512]{2,1,0:T(8,128)}, f32[2,128,512]{2,1,0:T(8,128)}, u32[]{:S(2)}, u32[]{:S(2)}) collective-permute-start(f32[2,128,512]{2,1,0:T(8,128)} %convolution_bitcast_fusion.2), channel_id=1, source_target_pairs={{0,4},{4,0},{8,12},{12,8},{16,20},{20,16},{24,28},{28,24},{1,5},{5... | collective-permute-start | bytes 1572872 | tf_op jit(solution)/shard_map/ppermute | solution.py:17
  44.7 14.7 %collective-permute-start.1 = (f32[2,128,512]{2,1,0:T(8,128)}, f32[2,128,512]{2,1,0:T(8,128)}, u32[]{:S(2)}, u32[]{:S(2)}) collective-permute-start(f32[2,128,512]{2,1,0:T(8,128)} %convolution_bitcast_fusion.1), channel_id=1, source_target_pairs={{0,8},{8,0},{4,12},{12,4},{16,24},{24,16},{20,28},{28,20},{1,9},{9... | collective-permute-start | bytes 1572872 | tf_op jit(solution)/shard_map/ppermute | solution.py:17
  47.9 14.4 %collective-permute-start.2 = (f32[2,128,512]{2,1,0:T(8,128)}, f32[2,128,512]{2,1,0:T(8,128)}, u32[]{:S(2)}, u32[]{:S(2)}) collective-permute-start(f32[2,128,512]{2,1,0:T(8,128)} %convolution_bitcast_fusion), channel_id=1, source_target_pairs={{0,16},{16,0},{4,20},{20,4},{8,24},{24,8},{12,28},{28,12},{1,17},{... | collective-permute-start | bytes 1572872 | tf_op jit(solution)/shard_map/ppermute | solution.py:17
  50.1 35.3 %copy-start.1 = (f32[256,512]{1,0:T(8,128)S(1)}, f32[256,512]{1,0:T(8,128)}, u32[]{:S(2)}) copy-start(f32[256,512]{1,0:T(8,128)} %param.10) | copy-start | bytes 1572868
  50.1 35.3 %copy-start.5 = (f32[256,512]{1,0:T(8,128)S(1)}, f32[256,512]{1,0:T(8,128)}, u32[]{:S(2)}) copy-start(f32[256,512]{1,0:T(8,128)} %param.11) | copy-start | bytes 1572868
Sparse Core Ops, SparseCore 0:
  12.4 27.2 all-gather.1
  42.0 43.3 reduce-scatter.1
where the time goes:
time: 94.6 us; the launch traced here: 94.3 us
  waiting for transfers between devices  52.2 us (55%)
  between operations  13.7 us (14%)
  matrix products  10.2 us (11%)
  starting transfers between devices  7.59 us (8%)
  local copies, waits for them, and re-layouts  7.1 us (8%)
  other arithmetic  3.41 us (4%)
    reduce_scatter x1, waiting for transfers between devices, on_device(): lax.psum_scatter(group_terms, 'qtr', scatter_dimension=0, tiled=True)  21.3 us
    all_gather x1, waiting for transfers between devices, on_device(): lax.all_gather(vec_bf, 'qtr', axis=0, tiled=True)  16.4 us
    ppermute x6, waiting for transfers between devices, from_partner(): return lax.ppermute(block, axis, route)  14.4 us
    ppermute x6, starting transfers between devices, from_partner(): return lax.ppermute(block, axis, route)  7.54 us
    dot_general x1, matrix products, on_device(): jnp.einsum('gcab,cbk->gak', spread_all, operand_all, preferred_element_ty...  3.76 us
    dot_general x3, matrix products, on_device(): jnp.einsum('csab,csak->cbk', off_live[partner], rows_picked, preferred_el...  3.55 us
    gather x3, local copies, waits for them, and re-layouts, on_device(): rows_picked = jnp.take(gathered, off_rows[partner], axis=0)  3.15 us
    sub x1, other arithmetic, on_device(): return 2.0 / cheb_half * (combined - cheb_center * vectors) - previous  2.02 us
  transfers between devices with their start and end apart: 8, of which 6 were waited for; matrix products, arithmetic and copies ran while one was open for 18% of the time, Pallas kernels for 0%

commit v1 on v0

v1 whole, which is shorter than its diff:
```python
import functools

import jax
import jax.numpy as jnp
from jax import lax
from jax.experimental import pallas as pl
from jax.experimental.pallas import tpu as pltpu
from jax.sharding import PartitionSpec as P

cheb_center = 0.25
cheb_half = 2.0
partners = 3
chunks = 2
MESH = pl.DeviceIdType.MESH
f32 = jnp.float32
bf16 = jnp.bfloat16


def flip(index, bit):
    step = 1 << bit
    return index + step - 2 * step * ((index // step) % 2)


def dot(left, right):
    return jnp.dot(left, right, preferred_element_type=f32)


def kernel(
    quarters, bit_list,
    dcols, dmask, orows, omask, vec_hbm, prev_hbm, diag_hbm, off_hbm,
    out,
    vec, prev, diag, off, tiles, tiles_t, w, wt, own, pvec, prod_out, prod_in,
    inbox, outbox, acc, terms,
    load_sem, z_send, z_recv, p_send, p_recv,
):
    Q = quarters
    g = lax.axis_index("grp")
    q = lax.axis_index("qtr")
    rows = own.shape[1]
    width = own.shape[2]
    tile = tiles.shape[-1]
    strips = rows // tile
    slots = diag.shape[1]
    has_left = q > 0
    has_right = q < Q - 1
    back = Q - 1 - q
    peers = [(flip(g, bit), q) for bit in bit_list]
    sides = ((g, q - 1), (g, q + 1))
    has_side = (has_left, has_right)

    loads = [
        pltpu.make_async_copy(src, dst, load_sem.at[i])
        for i, (src, dst) in enumerate(
            ((vec_hbm, vec), (diag_hbm, diag), (off_hbm, off), (prev_hbm, prev))
        )
    ]
    for load in loads:
        load.start()

    barrier = pltpu.get_barrier_semaphore()
    for peer in peers:
        pl.semaphore_signal(barrier, inc=1, device_id=peer, device_id_type=MESH)
    for side in range(2):
        @pl.when(has_side[side])
        def _():
            pl.semaphore_signal(barrier, inc=1, device_id=sides[side], device_id_type=MESH)

    loads[0].wait()
    for c in range(chunks):
        own[c] = vec[:, c * width:(c + 1) * width].astype(bf16)

    neighbours = jnp.where(has_left, 1, 0) + jnp.where(has_right, 1, 0)
    pl.semaphore_wait(barrier, partners + neighbours)

    def z_copy(src, to_right, idx, c):
        lane = 0 if to_right else 1
        return pltpu.make_async_remote_copy(
            src_ref=src,
            dst_ref=inbox.at[lane, idx, c],
            send_sem=z_send.at[lane, idx, c],
            recv_sem=z_recv.at[lane, idx, c],
            device_id=sides[1 if to_right else 0],
            device_id_type=MESH,
        )

    def p_copy(kind, j, c):
        return pltpu.make_async_remote_copy(
            src_ref=own.at[c] if kind == 0 else prod_out.at[j, c],
            dst_ref=pvec.at[j, c] if kind == 0 else prod_in.at[j, c],
            send_sem=p_send.at[kind, j, c],
            recv_sem=p_recv.at[kind, j, c],
            device_id=peers[j],
            device_id_type=MESH,
        )

    for c in range(chunks):
        @pl.when(has_right)
        def _():
            z_copy(own.at[c], True, 0, c).start()

        @pl.when(has_left)
        def _():
            z_copy(own.at[c], False, 0, c).start()

        for j in reversed(range(partners)):
            p_copy(0, j, c).start()

    loads[1].wait()
    loads[2].wait()
    zero = jnp.zeros((tile, tile), bf16)
    blocks = strips * (1 + partners)
    for n in range(blocks):
        tiles[n, 0] = zero
        tiles_t[n, 0] = zero
        for s in range(slots):
            if n < strips:
                block = diag[n, s]
                tiles[n, s + 1] = block.T
                tiles_t[n, s + 1] = block
            else:
                block = off[n // strips - 1, n % strips, s]
                tiles[n, s + 1] = block
                tiles_t[n, s + 1] = block.T
    for n in range(blocks):
        if n < strips:
            targets = [dcols[n, s] for s in range(slots)]
            flags = [dmask[n, s] * (s + 1) for s in range(slots)]
        else:
            j, k = n // strips - 1, n % strips
            targets = [orows[j, k, s] for s in range(slots)]
            flags = [omask[j, k, s] * (s + 1) for s in range(slots)]
        for r in range(strips * Q):
            place = jnp.int32(0)
            for s in range(slots):
                place = place + jnp.where(targets[s] == r, flags[s], 0)
            d, k = r // strips, r % strips
            w[d, k * tile:(k + 1) * tile, n * tile:(n + 1) * tile] = tiles[n, place]
            wt[d, n * tile:(n + 1) * tile, k * tile:(k + 1) * tile] = tiles_t[n, place]

    def gather_step(idx, c):
        for side, count, src in ((0, q, q - 1 - idx), (1, back, q + 1 + idx)):
            @pl.when(idx < count)
            def _():
                acc[c] += dot(wt[src], inbox[side, idx, c])

    for idx in range(Q):
        for c in range(chunks):
            for side, count in ((0, q), (1, back)):
                to_right = side == 0

                @pl.when(has_side[side])
                def _():
                    z_copy(outbox.at[side, idx, c], to_right, idx, c).wait_recv()

                if idx < Q - 1:
                    @pl.when((idx < count) & has_side[1 - side])
                    def _():
                        z_copy(inbox.at[side, idx, c], to_right, idx + 1, c).start()

            if idx == 0:
                for j in range(partners):
                    p_copy(0, j, c).wait_recv()
                for d in range(Q):
                    total = dot(w[d, :, :rows], own[c])
                    for j in range(partners):
                        total += dot(w[d, :, (j + 1) * rows:(j + 2) * rows], pvec[j, c])
                    terms[d, c] = total

            if idx < Q - 1:
                for side, count in ((0, q), (1, back)):
                    to_right = side == 0
                    dest = Q - 1 - idx + q if to_right else idx - back

                    @pl.when((idx >= count) & has_side[1 - side] & has_side[side])
                    def _():
                        outbox[side, idx + 1, c] = (
                            terms[dest, c] + inbox[side, idx, c].astype(f32)
                        ).astype(bf16)

                    @pl.when((idx >= count) & has_side[1 - side] & (count == 0))
                    def _():
                        outbox[side, idx + 1, c] = terms[dest, c].astype(bf16)

                    @pl.when((idx >= count) & has_side[1 - side])
                    def _():
                        z_copy(outbox.at[side, idx + 1, c], to_right, idx + 1, c).start()

            if idx == 0:
                acc[c] = dot(wt[q], own[c])
            if idx < Q - 1:
                gather_step(idx, c)
                last = jnp.maximum(q, back) - 1

                @pl.when(idx == last)
                def _():
                    for j in reversed(range(partners)):
                        prod_out[j, c] = acc[c, (j + 1) * rows:(j + 2) * rows].astype(bf16)
                        p_copy(1, j, c).start()

            if idx == Q - 1:
                if c == 0:
                    loads[3].wait()
                total = acc[c, :rows] + terms[q, c]
                for j in range(partners):
                    p_copy(1, j, c).wait_recv()
                    total += prod_in[j, c].astype(f32)
                acc[c, :rows] = total
                for side in range(2):
                    @pl.when(has_side[side])
                    def _():
                        acc[c, :rows] += inbox[side, idx, c].astype(f32)
                cols = slice(c * width, (c + 1) * width)
                out[:, cols] = (
                    2.0 / cheb_half * (acc[c, :rows] - cheb_center * vec[:, cols]) - prev[:, cols]
                )

    for c in range(chunks):
        for kind in range(2):
            for j in range(partners):
                p_copy(kind, j, c).wait_send()
        for idx in range(Q):
            for side in range(2):
                @pl.when(has_side[1 - side])
                def _():
                    z_copy(outbox.at[side, idx, c], side == 0, idx, c).wait_send()


def on_device(vectors, previous, diag_tiles, diag_cols, diag_mask, off_tiles, off_rows, off_mask):
    tile = diag_tiles.shape[-1]
    strips, slots = diag_tiles.shape[:2]
    rows, vec_width = vectors.shape
    quarters = lax.axis_size("qtr")
    levels = lax.axis_size("grp").bit_length() - 1
    bit_list = (0, levels // 2, levels - 1)
    width = vec_width // chunks
    blocks = strips * (1 + partners)
    whole = blocks * tile
    smem = pl.BlockSpec(memory_space=pltpu.SMEM)
    hbm = pl.BlockSpec(memory_space=pl.ANY)
    dma = pltpu.SemaphoreType.DMA
    macs = 2 * whole * quarters * rows * vec_width
    return pl.pallas_call(
        functools.partial(kernel, quarters, bit_list),
        out_shape=jax.ShapeDtypeStruct((rows, vec_width), f32),
        in_specs=[smem] * 4 + [hbm] * 4,
        out_specs=pl.BlockSpec(memory_space=pltpu.VMEM),
        scratch_shapes=[
            pltpu.VMEM((rows, vec_width), f32),
            pltpu.VMEM((rows, vec_width), f32),
            pltpu.VMEM(diag_tiles.shape, bf16),
            pltpu.VMEM(off_tiles.shape, bf16),
            pltpu.VMEM((blocks, slots + 1, tile, tile), bf16),
            pltpu.VMEM((blocks, slots + 1, tile, tile), bf16),
            pltpu.VMEM((quarters, rows, whole), bf16),
            pltpu.VMEM((quarters, whole, rows), bf16),
            pltpu.VMEM((chunks, rows, width), bf16),
            pltpu.VMEM((partners, chunks, rows, width), bf16),
            pltpu.VMEM((partners, chunks, rows, width), bf16),
            pltpu.VMEM((partners, chunks, rows, width), bf16),
            pltpu.VMEM((2, quarters, chunks, rows, width), bf16),
            pltpu.VMEM((2, quarters, chunks, rows, width), bf16),
            pltpu.VMEM((chunks, whole, width), f32),
            pltpu.VMEM((quarters, chunks, rows, width), f32),
            dma((4,)),
            dma((2, quarters, chunks)),
            dma((2, quarters, chunks)),
            dma((2, partners, chunks)),
            dma((2, partners, chunks)),
        ],
        compiler_params=pltpu.CompilerParams(
            collective_id=0, has_side_effects=True, vmem_limit_bytes=48 << 20
        ),
        cost_estimate=pl.CostEstimate(
            flops=2 * macs, bytes_accessed=4 * rows * vec_width * 4, transcendentals=0
        ),
    )(diag_cols, diag_mask, off_rows, off_mask, vectors, previous, diag_tiles, off_tiles)


def solution(mesh):
    in_specs = (
        P(("grp", "qtr"), None),
        P(("grp", "qtr"), None),
        P(("grp", "qtr"), None, None, None),
        P(("grp", "qtr"), None),
        P(("grp", "qtr"), None),
        P(None, ("grp", "qtr"), None, None, None),
        P(None, ("grp", "qtr"), None),
        P(None, ("grp", "qtr"), None),
    )
    out_specs = P(("grp", "qtr"), None)
    return jax.shard_map(
        on_device, mesh=mesh, in_specs=in_specs, out_specs=out_specs, check_vma=False
    )
```

time: 94.6 us -> 37.9 us (0.40)
  waiting for transfers between devices: 52.2 us -> 0 us
  Pallas kernels: 0 us -> 29.8 us
  between operations: 13.7 us -> 0.02 us
  matrix products: 10.2 us -> 0 us
  starting transfers between devices: 7.59 us -> 0 us
  other arithmetic: 3.41 us -> 0 us
    pallas_call x0 -> x1, Pallas kernels: none -> 29.8 us  [on_device(): pl.pallas_call(functools.partial(kernel, quarters, bit_list), out_shape=j...]
    reduce_scatter x1 -> x0, waiting for transfers between devices: 21.3 us -> none  [on_device(): lax.psum_scatter(group_terms, 'qtr', scatter_dimension=0, tiled=True)]
    all_gather x1 -> x0, waiting for transfers between devices: 16.4 us -> none  [on_device(): lax.all_gather(vec_bf, 'qtr', axis=0, tiled=True)]
    ppermute x6 -> x0, waiting for transfers between devices: 14.4 us -> none  [from_partner(): return lax.ppermute(block, axis, route)]
    dot_general x9 -> x0, matrix products: 10.2 us -> none  [the longest x1 3.76 us: on_device(): jnp.einsum('gcab,cbk->gak', spread_all, operand_all, preferred_element_ty...]
    ppermute x6 -> x0, starting transfers between devices: 7.54 us -> none  [from_partner(): return lax.ppermute(block, axis, route)]
    unnamed x21 -> x17, local copies, waits for them, and re-layouts: 1.82 us -> 7.68 us
    gather x4 -> x0, local copies, waits for them, and re-layouts: 3.76 us -> none  [the longest x3 3.15 us: on_device(): rows_picked = jnp.take(gathered, off_rows[partner], axis=0)]
  transfers between devices with their start and end apart: 8 -> 0, of which waited for: 6 -> 0; matrix products, arithmetic and copies ran while one was open for 18% -> 0% of each run, Pallas kernels for 0% -> 0%
where the time goes in v1:
time: 37.9 us; the launch traced here: 37.5 us
  Pallas kernels  29.8 us (79%)
  local copies, waits for them, and re-layouts  7.68 us (20%)
    pallas_call x1, Pallas kernels, on_device(): pl.pallas_call(functools.partial(kernel, quarters, bit_list), out_shape=j...  29.8 us
    unnamed x17, local copies, waits for them, and re-layouts  7.68 us

profile of v1, /device:TPU:0, one launch (start us, length us, event | category | flops | bytes accessed | tf_op | source)
XLA Modules:
  0.0 37.5 jit_solution(5079539786718893354)
XLA Ops:
  0.0 0.0 copy-start
  0.0 1.1 %copy-done = bf16[3,2,4,128,128]{4,3,2,1,0:T(8,128)(2,1)S(1)} copy-done((bf16[3,2,4,128,128]{4,3,2,1,0:T(8,128)(2,1)S(1)}, bf16[3,2,4,128,128]{4,3,2,1,0:T(8,128)(2,1)}, u32[]{:S(2)}) %copy-start) | copy-done | bytes 786456
  1.1 0.0 copy-start.1
  1.1 1.0 %copy-done.1 = f32[256,512]{1,0:T(8,128)S(1)} copy-done((f32[256,512]{1,0:T(8,128)S(1)}, f32[256,512]{1,0:T(8,128)}, u32[]{:S(2)}) %copy-start.1) | copy-done | bytes 524312
  2.2 0.0 copy-start.2
  2.2 1.0 %copy-done.2 = f32[256,512]{1,0:T(8,128)S(1)} copy-done((f32[256,512]{1,0:T(8,128)S(1)}, f32[256,512]{1,0:T(8,128)}, u32[]{:S(2)}) %copy-start.2) | copy-done | bytes 524312
  3.2 0.0 copy-start.3
  3.2 0.9 %copy-done.3 = bf16[2,4,128,128]{3,2,1,0:T(8,128)(2,1)S(1)} copy-done((bf16[2,4,128,128]{3,2,1,0:T(8,128)(2,1)S(1)}, bf16[2,4,128,128]{3,2,1,0:T(8,128)(2,1)}, u32[]{:S(2)}) %copy-start.3) | copy-done | bytes 262168
  4.2 0.0 copy-start.4
  4.2 0.7 %copy-done.4 = s32[3,2,4]{2,1,0:T(2,128)S(1)} copy-done((s32[3,2,4]{2,1,0:T(2,128)S(1)}, s32[3,2,4]{2,1,0:T(2,128)}, u32[]{:S(2)}) %copy-start.4) | copy-done | bytes 120
  4.9 0.0 copy-start.5
  4.9 0.7 %copy-done.5 = s32[3,2,4]{2,1,0:T(2,128)S(1)} copy-done((s32[3,2,4]{2,1,0:T(2,128)S(1)}, s32[3,2,4]{2,1,0:T(2,128)}, u32[]{:S(2)}) %copy-start.5) | copy-done | bytes 120
  5.5 0.0 copy-start.6
  5.5 0.7 %copy-done.6 = s32[2,4]{1,0:T(2,128)S(1)} copy-done((s32[2,4]{1,0:T(2,128)S(1)}, s32[2,4]{1,0:T(2,128)}, u32[]{:S(2)}) %copy-start.6) | copy-done | bytes 56
  6.2 0.0 copy-start.7
  6.2 0.7 %copy-done.7 = s32[2,4]{1,0:T(2,128)S(1)} copy-done((s32[2,4]{1,0:T(2,128)S(1)}, s32[2,4]{1,0:T(2,128)}, u32[]{:S(2)}) %copy-start.7) | copy-done | bytes 56
  6.9 29.8 %shard_map.82 = f32[256,512]{1,0:T(8,128)S(1)} custom-call(s32[2,4]{1,0:T(2,128)S(1)} %copy-done.6, s32[2,4]{1,0:T(2,128)S(1)} %copy-done.7, s32[3,2,4]{2,1,0:T(2,128)S(1)} %copy-done.4, s32[3,2,4]{2,1,0:T(2,128)S(1)} %copy-done.5, f32[256,512]{1,0:T(8,128)S(1)} %copy-done.1, f32[256,512]{1,0:T(8,128)S(1)} %copy-done.2, ...), custom_call_target="tpu_custom_call" | custom-call | flops 2147483648 | bytes 2097152 | tf_op jit(solution)/shard_map/pallas_call | solution.py:242
  36.7 0.8 %copy.10 = f32[256,512]{1,0:T(8,128)} copy(f32[256,512]{1,0:T(8,128)S(1)} %shard_map.82) | data formatting | bytes 1048576
Async XLA Ops:
  0.0 1.1 %copy-start = (bf16[3,2,4,128,128]{4,3,2,1,0:T(8,128)(2,1)S(1)}, bf16[3,2,4,128,128]{4,3,2,1,0:T(8,128)(2,1)}, u32[]{:S(2)}) copy-start(bf16[3,2,4,128,128]{4,3,2,1,0:T(8,128)(2,1)} %off_hbm.1) | copy-start | bytes 2359300
  1.1 1.0 %copy-start.1 = (f32[256,512]{1,0:T(8,128)S(1)}, f32[256,512]{1,0:T(8,128)}, u32[]{:S(2)}) copy-start(f32[256,512]{1,0:T(8,128)} %vec_hbm.1) | copy-start | bytes 1572868
  2.2 1.0 %copy-start.2 = (f32[256,512]{1,0:T(8,128)S(1)}, f32[256,512]{1,0:T(8,128)}, u32[]{:S(2)}) copy-start(f32[256,512]{1,0:T(8,128)} %prev_hbm.1) | copy-start | bytes 1572868
  3.2 0.9 %copy-start.3 = (bf16[2,4,128,128]{3,2,1,0:T(8,128)(2,1)S(1)}, bf16[2,4,128,128]{3,2,1,0:T(8,128)(2,1)}, u32[]{:S(2)}) copy-start(bf16[2,4,128,128]{3,2,1,0:T(8,128)(2,1)} %diag_hbm.1) | copy-start | bytes 786436
  4.2 0.7 %copy-start.4 = (s32[3,2,4]{2,1,0:T(2,128)S(1)}, s32[3,2,4]{2,1,0:T(2,128)}, u32[]{:S(2)}) copy-start(s32[3,2,4]{2,1,0:T(2,128)} %orows.1) | copy-start | bytes 292
  4.9 0.7 %copy-start.5 = (s32[3,2,4]{2,1,0:T(2,128)S(1)}, s32[3,2,4]{2,1,0:T(2,128)}, u32[]{:S(2)}) copy-start(s32[3,2,4]{2,1,0:T(2,128)} %omask.1) | copy-start | bytes 292
  5.5 0.7 %copy-start.6 = (s32[2,4]{1,0:T(2,128)S(1)}, s32[2,4]{1,0:T(2,128)}, u32[]{:S(2)}) copy-start(s32[2,4]{1,0:T(2,128)} %dcols.1) | copy-start | bytes 100
  6.2 0.7 %copy-start.7 = (s32[2,4]{1,0:T(2,128)S(1)}, s32[2,4]{1,0:T(2,128)}, u32[]{:S(2)}) copy-start(s32[2,4]{1,0:T(2,128)} %dmask.1) | copy-start | bytes 100

commit v2 on v1

v2 whole, which is shorter than its diff:
```python
import functools

import jax
import jax.numpy as jnp
from jax import lax
from jax.experimental import pallas as pl
from jax.experimental.pallas import tpu as pltpu
from jax.sharding import PartitionSpec as P

cheb_center = 0.25
cheb_half = 2.0
partners = 3
chunks = 2
MESH = pl.DeviceIdType.MESH
f32 = jnp.float32
bf16 = jnp.bfloat16


def flip(index, bit):
    step = 1 << bit
    return index + step - 2 * step * ((index // step) % 2)


def dot(left, right):
    return jnp.dot(left, right, preferred_element_type=f32)


def kernel(
    quarters, bit_list,
    dcols_hbm, dmask_hbm, orows_hbm, omask_hbm, vec_hbm, prev_hbm, diag_hbm, off_hbm,
    out,
    dcols, dmask, orows, omask, vec, prev, diag, off, tiles, tiles_t, w, wt, own, pvec, prod_out, prod_in,
    inbox, outbox, acc, terms,
    load_sem, z_send, z_recv, p_send, p_recv,
):
    Q = quarters
    g = lax.axis_index("grp")
    q = lax.axis_index("qtr")
    rows = own.shape[1]
    width = own.shape[2]
    tile = tiles.shape[-1]
    strips = rows // tile
    slots = diag.shape[1]
    has_left = q > 0
    has_right = q < Q - 1
    back = Q - 1 - q
    peers = [(flip(g, bit), q) for bit in bit_list]
    sides = ((g, q - 1), (g, q + 1))
    has_side = (has_left, has_right)

    loads = [
        pltpu.make_async_copy(src, dst, load_sem.at[i])
        for i, (src, dst) in enumerate(
            (
                (vec_hbm, vec), (dcols_hbm, dcols), (dmask_hbm, dmask), (orows_hbm, orows),
                (omask_hbm, omask), (diag_hbm, diag), (off_hbm, off), (prev_hbm, prev),
            )
        )
    ]
    for load in loads:
        load.start()

    barrier = pltpu.get_barrier_semaphore()
    for peer in peers:
        pl.semaphore_signal(barrier, inc=1, device_id=peer, device_id_type=MESH)
    for side in range(2):
        @pl.when(has_side[side])
        def _():
            pl.semaphore_signal(barrier, inc=1, device_id=sides[side], device_id_type=MESH)

    loads[0].wait()
    for c in range(chunks):
        own[c] = vec[:, c * width:(c + 1) * width].astype(bf16)

    neighbours = jnp.where(has_left, 1, 0) + jnp.where(has_right, 1, 0)
    pl.semaphore_wait(barrier, partners + neighbours)

    def z_copy(src, to_right, idx, c, h):
        lane = 0 if to_right else 1
        part = pl.ds(h * tile, tile)
        return pltpu.make_async_remote_copy(
            src_ref=src.at[part],
            dst_ref=inbox.at[lane, idx, c, part],
            send_sem=z_send.at[lane, idx, c, h],
            recv_sem=z_recv.at[lane, idx, c, h],
            device_id=sides[1 if to_right else 0],
            device_id_type=MESH,
        )

    def p_copy(kind, j, c):
        return pltpu.make_async_remote_copy(
            src_ref=own.at[c] if kind == 0 else prod_out.at[j, c],
            dst_ref=pvec.at[j, c] if kind == 0 else prod_in.at[j, c],
            send_sem=p_send.at[kind, j, c],
            recv_sem=p_recv.at[kind, j, c],
            device_id=peers[j],
            device_id_type=MESH,
        )

    for c in range(chunks):
        for h in range(strips):
            @pl.when(has_right)
            def _():
                z_copy(own.at[c], True, 0, c, h).start()

            @pl.when(has_left)
            def _():
                z_copy(own.at[c], False, 0, c, h).start()

        for j in reversed(range(partners)):
            p_copy(0, j, c).start()

    for load in loads[1:7]:
        load.wait()
    zero = jnp.zeros((tile, tile), bf16)
    blocks = strips * (1 + partners)

    def block_of(n, s):
        return diag[n, s] if n < strips else off[n // strips - 1, n % strips, s]

    def places(n):
        if n < strips:
            targets = [dcols[n, s] for s in range(slots)]
            flags = [dmask[n, s] * (s + 1) for s in range(slots)]
        else:
            j, k = n // strips - 1, n % strips
            targets = [orows[j, k, s] for s in range(slots)]
            flags = [omask[j, k, s] * (s + 1) for s in range(slots)]
        for r in range(strips * Q):
            place = jnp.int32(0)
            for s in range(slots):
                place = place + jnp.where(targets[s] == r, flags[s], 0)
            yield r // strips, (r % strips) * tile, place

    def fill(held, across, put):
        for n in range(blocks):
            held[n, 0] = zero
            for s in range(slots):
                block = block_of(n, s)
                held[n, s + 1] = block.T if (n < strips) == across else block
        for n in range(blocks):
            for d, low, place in places(n):
                put(d, low, n * tile, held[n, place])

    def put_w(d, low, col, block):
        w[d, low:low + tile, col:col + tile] = block

    def put_wt(d, low, col, block):
        wt[d, col:col + tile, low:low + tile] = block

    fill(tiles, True, put_w)

    def gather_step(idx, c):
        for side, count, src in ((0, q, q - 1 - idx), (1, back, q + 1 + idx)):
            @pl.when(idx < count)
            def _():
                acc[c] += dot(wt[src], inbox[side, idx, c])

    def arrive(idx, c, h):
        for side, count in ((0, q), (1, back)):
            to_right = side == 0

            @pl.when(has_side[side])
            def _():
                z_copy(outbox.at[side, idx, c], to_right, idx, c, h).wait_recv()

            if idx < Q - 1:
                @pl.when((idx < count) & has_side[1 - side])
                def _():
                    z_copy(inbox.at[side, idx, c], to_right, idx + 1, c, h).start()

    def reduce_on(idx, c, h):
        part = slice(h * tile, (h + 1) * tile)
        for side, count in ((0, q), (1, back)):
            to_right = side == 0
            dest = Q - 1 - idx + q if to_right else idx - back
            goes = (idx >= count) & has_side[1 - side]

            @pl.when(goes & has_side[side])
            def _():
                outbox[side, idx + 1, c, part] = (
                    terms[dest, c, part] + inbox[side, idx, c, part].astype(f32)
                ).astype(bf16)

            @pl.when(goes & (count == 0))
            def _():
                outbox[side, idx + 1, c, part] = terms[dest, c, part].astype(bf16)

            @pl.when(goes)
            def _():
                z_copy(outbox.at[side, idx + 1, c], to_right, idx + 1, c, h).start()

    for c in range(chunks):
        for h in range(strips):
            arrive(0, c, h)
        for j in range(partners):
            p_copy(0, j, c).wait_recv()
        for d in range(Q):
            total = dot(w[d, :, :rows], own[c])
            for j in range(partners):
                total += dot(w[d, :, (j + 1) * rows:(j + 2) * rows], pvec[j, c])
            terms[d, c] = total
        for h in range(strips):
            reduce_on(0, c, h)

    fill(tiles_t, False, put_wt)

    for idx in range(1, Q - 1):
        for c in range(chunks):
            for h in range(strips):
                arrive(idx, c, h)
                reduce_on(idx, c, h)
            if idx == 1:
                acc[c] = dot(wt[q], own[c])
                gather_step(0, c)
            gather_step(idx, c)
            last = jnp.maximum(jnp.maximum(q, back) - 1, 1)

            @pl.when(idx == last)
            def _():
                for j in reversed(range(partners)):
                    prod_out[j, c] = acc[c, (j + 1) * rows:(j + 2) * rows].astype(bf16)
                    p_copy(1, j, c).start()

    loads[7].wait()
    for c in range(chunks):
        cols = slice(c * width, (c + 1) * width)
        total = acc[c, :rows] + terms[q, c]
        for j in range(partners):
            p_copy(1, j, c).wait_recv()
            total += prod_in[j, c].astype(f32)
        out[:, cols] = 2.0 / cheb_half * (total - cheb_center * vec[:, cols]) - prev[:, cols]
        for h in range(strips):
            part = slice(h * tile, (h + 1) * tile)
            arrive(Q - 1, c, h)
            for side in range(2):
                @pl.when(has_side[side])
                def _():
                    out[part, cols] += 2.0 / cheb_half * inbox[side, Q - 1, c, part].astype(f32)

    for c in range(chunks):
        for kind in range(2):
            for j in range(partners):
                p_copy(kind, j, c).wait_send()
        for idx in range(Q):
            for h in range(strips):
                for side in range(2):
                    @pl.when(has_side[1 - side])
                    def _():
                        z_copy(outbox.at[side, idx, c], side == 0, idx, c, h).wait_send()


def on_device(vectors, previous, diag_tiles, diag_cols, diag_mask, off_tiles, off_rows, off_mask):
    tile = diag_tiles.shape[-1]
    strips, slots = diag_tiles.shape[:2]
    rows, vec_width = vectors.shape
    quarters = lax.axis_size("qtr")
    levels = lax.axis_size("grp").bit_length() - 1
    bit_list = (0, levels // 2, levels - 1)
    width = vec_width // chunks
    blocks = strips * (1 + partners)
    whole = blocks * tile
    hbm = pl.BlockSpec(memory_space=pltpu.HBM)
    dma = pltpu.SemaphoreType.DMA
    macs = 2 * whole * quarters * rows * vec_width
    return pl.pallas_call(
        functools.partial(kernel, quarters, bit_list),
        out_shape=jax.ShapeDtypeStruct((rows, vec_width), f32),
        in_specs=[hbm] * 8,
        out_specs=pl.BlockSpec(memory_space=pltpu.VMEM),
        scratch_shapes=[
            pltpu.SMEM(diag_cols.shape, jnp.int32),
            pltpu.SMEM(diag_mask.shape, jnp.int32),
            pltpu.SMEM(off_rows.shape, jnp.int32),
            pltpu.SMEM(off_mask.shape, jnp.int32),
            pltpu.VMEM((rows, vec_width), f32),
            pltpu.VMEM((rows, vec_width), f32),
            pltpu.VMEM(diag_tiles.shape, bf16),
            pltpu.VMEM(off_tiles.shape, bf16),
            pltpu.VMEM((blocks, slots + 1, tile, tile), bf16),
            pltpu.VMEM((blocks, slots + 1, tile, tile), bf16),
            pltpu.VMEM((quarters, rows, whole), bf16),
            pltpu.VMEM((quarters, whole, rows), bf16),
            pltpu.VMEM((chunks, rows, width), bf16),
            pltpu.VMEM((partners, chunks, rows, width), bf16),
            pltpu.VMEM((partners, chunks, rows, width), bf16),
            pltpu.VMEM((partners, chunks, rows, width), bf16),
            pltpu.VMEM((2, quarters, chunks, rows, width), bf16),
            pltpu.VMEM((2, quarters, chunks, rows, width), bf16),
            pltpu.VMEM((chunks, whole, width), f32),
            pltpu.VMEM((quarters, chunks, rows, width), f32),
            dma((8,)),
            dma((2, quarters, chunks, strips)),
            dma((2, quarters, chunks, strips)),
            dma((2, partners, chunks)),
            dma((2, partners, chunks)),
        ],
        compiler_params=pltpu.CompilerParams(
            collective_id=0, has_side_effects=True, vmem_limit_bytes=64 << 20
        ),
        cost_estimate=pl.CostEstimate(
            flops=2 * macs, bytes_accessed=4 * rows * vec_width * 4, transcendentals=0
        ),
    )(diag_cols, diag_mask, off_rows, off_mask, vectors, previous, diag_tiles, off_tiles)


def solution(mesh):
    in_specs = (
        P(("grp", "qtr"), None),
        P(("grp", "qtr"), None),
        P(("grp", "qtr"), None, None, None),
        P(("grp", "qtr"), None),
        P(("grp", "qtr"), None),
        P(None, ("grp", "qtr"), None, None, None),
        P(None, ("grp", "qtr"), None),
        P(None, ("grp", "qtr"), None),
    )
    out_specs = P(("grp", "qtr"), None)
    return jax.shard_map(
        on_device, mesh=mesh, in_specs=in_specs, out_specs=out_specs, check_vma=False
    )
```

time: 37.9 us -> 31.7 us (0.84)
  local copies, waits for them, and re-layouts: 7.68 us -> 1.87 us
    unnamed x17 -> x1, local copies, waits for them, and re-layouts: 7.68 us -> 1.87 us
where the time goes in v2:
time: 31.7 us; the launch traced here: 31.5 us
  Pallas kernels  29.6 us (93%)
  local copies, waits for them, and re-layouts  1.87 us (6%)
    pallas_call x1, Pallas kernels, on_device(): pl.pallas_call(functools.partial(kernel, quarters, bit_list), out_shape=j...  29.6 us
    unnamed x1, local copies, waits for them, and re-layouts  1.87 us

profile of v2, /device:TPU:0, one launch (start us, length us, event | category | flops | bytes accessed | tf_op | source)
XLA Modules:
  0.0 31.5 jit_solution(11699108570619972653)
XLA Ops:
  0.0 29.6 %shard_map.82 = f32[256,512]{1,0:T(8,128)} custom-call(s32[2,4]{1,0:T(2,128)} %dcols_hbm.1, s32[2,4]{1,0:T(2,128)} %dmask_hbm.1, s32[3,2,4]{2,1,0:T(2,128)} %orows_hbm.1, s32[3,2,4]{2,1,0:T(2,128)} %omask_hbm.1, f32[256,512]{1,0:T(8,128)} %vec_hbm.1, f32[256,512]{1,0:T(8,128)} %prev_hbm.1, bf16[2,4,128,128]{3,2,1,0:T(8,128)(2,1)} %diag_hbm.1, ...), custom_call_target="tpu_custom_call" | custom-call | flops 2147483648 | bytes 2097152 | tf_op jit(solution)/shard_map/pallas_call | solution.py:266
  29.6 1.9 %copy.10 = f32[256,512]{1,0:T(8,128)} copy(f32[256,512]{1,0:T(8,128)} %shard_map.82) | data formatting | bytes 1048576

commit v3 on v2

--- a/solution.py
+++ b/solution.py
@@ -97,7 +97,7 @@
             device_id_type=MESH,
         )
 
-    for c in range(chunks):
+    def send_own(c):
         for h in range(strips):
             @pl.when(has_right)
             def _():
@@ -109,6 +109,8 @@
 
         for j in reversed(range(partners)):
             p_copy(0, j, c).start()
+
+    send_own(0)
 
     for load in loads[1:7]:
         load.wait()
@@ -138,6 +140,9 @@
             for s in range(slots):
                 block = block_of(n, s)
                 held[n, s + 1] = block.T if (n < strips) == across else block
+        if across:
+            for c in range(1, chunks):
+                send_own(c)
         for n in range(blocks):
             for d, low, place in places(n):
                 put(d, low, n * tile, held[n, place])

time: 31.7 us -> 31.7 us (level)
  no operation moved by 1% of the time
where the time goes in v3:
time: 31.7 us; the launch traced here: 31.5 us
  Pallas kernels  29.6 us (93%)
  local copies, waits for them, and re-layouts  1.87 us (6%)
    pallas_call x1, Pallas kernels, on_device(): pl.pallas_call(functools.partial(kernel, quarters, bit_list), out_shape=j...  29.6 us
    unnamed x1, local copies, waits for them, and re-layouts  1.87 us

profile of v3, /device:TPU:0, one launch (start us, length us, event | category | flops | bytes accessed | tf_op | source)
XLA Modules:
  0.0 31.5 jit_solution(10140884456663696736)
XLA Ops:
  0.0 29.6 %shard_map.82 = f32[256,512]{1,0:T(8,128)} custom-call(s32[2,4]{1,0:T(2,128)} %dcols_hbm.1, s32[2,4]{1,0:T(2,128)} %dmask_hbm.1, s32[3,2,4]{2,1,0:T(2,128)} %orows_hbm.1, s32[3,2,4]{2,1,0:T(2,128)} %omask_hbm.1, f32[256,512]{1,0:T(8,128)} %vec_hbm.1, f32[256,512]{1,0:T(8,128)} %prev_hbm.1, bf16[2,4,128,128]{3,2,1,0:T(8,128)(2,1)} %diag_hbm.1, ...), custom_call_target="tpu_custom_call" | custom-call | flops 2147483648 | bytes 2097152 | tf_op jit(solution)/shard_map/pallas_call | solution.py:271
  29.6 1.9 %copy.10 = f32[256,512]{1,0:T(8,128)} copy(f32[256,512]{1,0:T(8,128)} %shard_map.82) | data formatting | bytes 1048576
